TPU v7x, 512 devices: a whole 4x8x8 slice. The times are simulated.
512 devices in a mesh: ctx: 32 (over x, y), tp: 16 (over z, core).
Axes of the slice: x: 4, y: 8, z: 8, core: 2. Of those that a mesh axis runs over, the one named last changes fastest.
Arguments:
- prefix_x: bfloat16 [8192, 8192], P('ctx', 'tp'), may hold values from -6 to 6
- prefix_z: bfloat16 [8192, 8192], P('ctx', 'tp'), may hold values from -6 to 6
- prefix_bc: bfloat16 [8192, 256], P(('ctx', 'tp')), may hold values from -6 to 6
- prefix_dt: float32 [128, 8192], P('tp', 'ctx'), may hold values from -6 to 6
- branch_x: bfloat16 [8192, 8192], P('ctx', 'tp'), may hold values from -6 to 6
- branch_z: bfloat16 [8192, 8192], P('ctx', 'tp'), may hold values from -6 to 6
- branch_bc: bfloat16 [8192, 256], P(('ctx', 'tp')), may hold values from -6 to 6
- branch_dt: float32 [128, 8192], P('tp', 'ctx'), may hold values from -6 to 6
- conv_x: bfloat16 [4, 8192], P(None, 'tp'), may hold values from -3 to 3
- conv_bc: bfloat16 [4, 256], replicated, may hold values from -3 to 3
- decay_rate: float32 [128], P('tp'), may hold values from 2.4414063e-05 to 0.03
- skip: float32 [128], P('tp'), may hold values from 0.5 to 1.5
- norm_gain: float32 [8192], P('tp'), may hold values from 0.5 to 1.5
- bound_pos: int32 [8], replicated, may hold values from 0 to 8191
- branch_owner: int32 [64], replicated, may hold values from 0 to 31, as said below
- branch_parent: int32 [64], replicated, may hold values from 0 to 7
- branch_len: int32 [64], replicated, may hold values from 1 to 255, as said below
Outputs:
- prefix_out: bfloat16 [8192, 8192], P('ctx', 'tp')
- branch_out: bfloat16 [8192, 8192], P('ctx', 'tp')
Inputs may be any that keep to these rules, and one draw needn't show every extreme that they name: `branch_owner`: every block index 0 to 31 holds exactly 2 branches. `branch_len`: the branches of one block have lengths that sum to at most 256; in every draw some block's sum is exactly 256, and some branch has exactly 255 rows.
All inputs are finite; a program needn't handle non-finite values.
Results may differ from a plain program's by a relative error of at most 0.0034.
Values may be sent and summed in bfloat16 or wider, within the bound.
No kernel may reach another device: no remote copies, remote signals or barrier semaphores. Data moves between devices by JAX's collectives and lax.ppermute only.
A program may use at most 64 MiB of HBM per device.

v0:
```python
import jax
import jax.numpy as jnp
from jax import lax
from jax.sharding import PartitionSpec as P

BR_PER = 2
EPSILON = 1e-05
SLOTS = 8
BF = jnp.bfloat16
F32 = jnp.float32
HIGH = lax.Precision.HIGHEST


def conv_silu(lagged, weights):
    summed = weights[0].astype(F32)[None, :] * lagged[0].astype(F32)
    for tap in range(1, len(lagged)):
        summed = summed + weights[tap].astype(F32)[None, :] * lagged[tap].astype(F32)
    return jax.nn.silu(summed).astype(BF)


def split_conv(convolved, channels, heads):
    length = convolved.shape[0]
    state = (convolved.shape[1] - channels) // 2
    values = convolved[:, :channels].reshape(length, heads, channels // heads)
    return (values, convolved[:, channels : channels + state], convolved[:, channels + state :])


def decays(raw_steps, rates):
    length = raw_steps.shape[1]
    step = jax.nn.softplus(raw_steps)
    log_decay = -rates[:, None] * step
    index = jnp.arange(length, dtype=jnp.int32)
    upper = (index[:, None] <= index[None, :]).astype(F32)
    return (step, log_decay, jnp.dot(log_decay, upper, precision=HIGH))


def intra(values, b_rows, c_rows, step, cumulative, mask):
    scores = jnp.dot(c_rows, b_rows.T, preferred_element_type=F32)
    exponent = jnp.where(mask[None], cumulative[:, :, None] - cumulative[:, None, :], 0.0)
    mixing = jnp.where(mask[None], scores[None] * jnp.exp(exponent) * step[:, None, :], 0.0)
    return jnp.einsum("hts,shp->thp", mixing.astype(BF), values, preferred_element_type=F32)


def pick(array, positions):
    index = jnp.arange(array.shape[1], dtype=jnp.int32)
    hit = index[None, None, :] == positions[:, None, None]
    return jnp.sum(jnp.where(hit, array[None], 0.0), axis=2)


def local_states(values, b_rows, step, cumulative, positions):
    length = cumulative.shape[1]
    ends = pick(cumulative, positions)
    row = jnp.arange(length, dtype=jnp.int32)
    inside = (row[None, :] <= positions[:, None])[:, None, :]
    exponent = jnp.where(inside, ends[:, :, None] - cumulative[None], 0.0)
    weight = jnp.where(inside, jnp.exp(exponent) * step[None], 0.0)
    weighted = (jnp.transpose(weight, (0, 2, 1))[:, :, :, None] * values[None].astype(F32)).astype(
        BF
    )
    states = jnp.einsum("jshp,sn->jhpn", weighted, b_rows, preferred_element_type=F32)
    return (states, ends)


def from_state(c_rows, state, weight):
    result = jnp.einsum("tn,hpn->thp", c_rows, state, preferred_element_type=F32)
    return result * weight.T[:, :, None]


def parts_of(value, count):
    found = []
    for _ in range(count):
        part = lax.reduce_precision(value, 8, 7)
        found.append(part.astype(BF))
        value = value - part
    return found


def body(
    prefix_x,
    prefix_z,
    prefix_bc,
    prefix_dt,
    branch_x,
    branch_z,
    branch_bc,
    branch_dt,
    conv_x,
    conv_bc,
    decay_rate,
    skip,
    norm_gain,
    bound_pos,
    branch_owner,
    branch_parent,
    branch_len,
):
    n_ctx = lax.axis_size("ctx")
    me = lax.axis_index("ctx")
    length, channels = prefix_x.shape
    heads = decay_rate.shape[0]
    width = prefix_bc.shape[1]
    n_state = width // 2
    bounds = bound_pos.shape[0]
    branches = branch_owner.shape[0]
    weights = jnp.concatenate([conv_x, conv_bc], axis=1)
    taps = weights.shape[0]
    tail = taps - 1
    row_width = channels + width
    gathered = lax.all_gather(
        jnp.concatenate([prefix_bc, branch_bc], axis=1), "tp", axis=0, tiled=True
    )
    joined = jnp.concatenate([prefix_x, gathered[:, :width]], axis=1)
    before = lax.ppermute(joined[length - tail :], "ctx", [(i, i + 1) for i in range(n_ctx - 1)])
    extended = jnp.concatenate([before, joined], axis=0)
    lagged = [extended[tap : tap + length] for tap in range(taps)]
    values, b_rows, c_rows = split_conv(conv_silu(lagged, weights), channels, heads)
    step, _, cumulative = decays(prefix_dt, decay_rate)
    block_of = bound_pos // length
    at = bound_pos - block_of * length
    order = jnp.arange(bounds, dtype=jnp.int32)
    slot_of = jnp.sum(
        ((block_of[:, None] == block_of[None, :]) & (order[None, :] < order[:, None])).astype(
            jnp.int32
        ),
        axis=1,
    )
    border = jnp.arange(branches, dtype=jnp.int32)
    same = branch_owner[:, None] == branch_owner[None, :]
    earlier = same & (border[None, :] < border[:, None])
    rank = jnp.sum(earlier.astype(jnp.int32), axis=1)
    start = jnp.sum(jnp.where(earlier, branch_len[None, :], 0), axis=1)
    place = jnp.arange(n_ctx * BR_PER, dtype=jnp.int32)
    chosen = place[:, None] == (branch_owner * BR_PER + rank)[None, :]
    parent_of = jnp.sum(jnp.where(chosen, branch_parent[None, :], 0), axis=1)
    mine = (me * BR_PER + jnp.arange(BR_PER, dtype=jnp.int32))[:, None] == (
        branch_owner * BR_PER + rank
    )[None, :]
    my_len = jnp.sum(jnp.where(mine, branch_len[None, :], 0), axis=1)
    my_start = jnp.sum(jnp.where(mine, start[None, :], 0), axis=1)
    slot_here = (block_of == me)[None, :] & (
        slot_of[None, :] == jnp.arange(SLOTS, dtype=jnp.int32)[:, None]
    )
    positions = jnp.sum(jnp.where(slot_here, at[None, :] + 1, 0), axis=1) - 1
    positions = jnp.concatenate([jnp.full((1,), length - 1, jnp.int32), positions])
    states, ends = local_states(values, b_rows, step, cumulative, positions)
    slices = states.reshape(SLOTS + 1, n_ctx, -1, n_state)
    rows = slices.shape[2]
    end_hi, end_lo = parts_of(slices[0], 2)
    partial = jnp.transpose(slices[1:].astype(BF), (1, 0, 2, 3)).reshape(
        n_ctx, SLOTS * rows, n_state
    )
    per_head = jnp.repeat(
        jnp.pad(ends.T, ((0, 0), (0, n_state - SLOTS - 1))), n_ctx // heads, axis=0
    )
    logs = jnp.stack(parts_of(per_head, 3), axis=1)
    parent_hit = parent_of[:, None] == order[None, :]
    parent_at = jnp.sum(jnp.where(parent_hit, at[None, :], 0), axis=1)
    parent_block = jnp.sum(jnp.where(parent_hit, block_of[None, :], 0), axis=1)
    wanted = parent_at[:, None] + 1 + jnp.arange(tail, dtype=jnp.int32)[None, :]
    wanted = jnp.where((parent_block == me)[:, None], wanted, -1).reshape(-1)
    picker = (wanted[:, None] == jnp.arange(length + tail, dtype=jnp.int32)[None, :]).astype(BF)
    tails = jnp.dot(picker, extended, preferred_element_type=F32).astype(BF)
    tails = tails.reshape(n_ctx, BR_PER * tail * row_width // n_state, n_state)
    pieces = [end_hi, end_lo, partial, tails, logs]
    sent = jnp.concatenate(pieces, axis=1)
    sent = jnp.pad(sent, ((0, 0), (0, -sent.shape[1] % 16), (0, 0)))
    got = lax.all_to_all(sent, "ctx", 0, 0, tiled=True)
    edges = [0]
    for piece in pieces:
        edges.append(edges[-1] + piece.shape[1])
    end_hi, end_lo, partial, tails, logs = [
        got[:, first:last].astype(F32) for first, last in zip(edges[:-1], edges[1:], strict=True)
    ]
    ends = jnp.sum(logs, axis=1)[:, : SLOTS + 1]
    block = jnp.arange(n_ctx, dtype=jnp.int32)
    totals = jnp.sum(jnp.where(block[None, :] <= block[:, None], ends[:, 0][None, :], 0.0), axis=1)
    gap = (totals - ends[:, 0])[:, None] - totals[None, :]
    earlier_block = block[None, :] < block[:, None]
    carry = jnp.where(earlier_block, jnp.exp(jnp.where(earlier_block, gap, 0.0)), 0.0)
    entering = jnp.dot(carry, (end_hi + end_lo).reshape(n_ctx, -1), precision=HIGH)
    held = block[None, :] == block_of[:, None]
    bound_end = jnp.sum(
        jnp.where(
            held[:, :, None]
            & (slot_of[:, None, None] == jnp.arange(SLOTS, dtype=jnp.int32)[None, None, :]),
            ends[None, :, 1:],
            0.0,
        ),
        axis=(1, 2),
    )
    choose = jnp.where(held, jnp.exp(bound_end)[:, None], 0.0)
    slot_pick = (
        held[:, :, None]
        & (slot_of[:, None, None] == jnp.arange(SLOTS, dtype=jnp.int32)[None, None, :])
    ).reshape(bounds, -1)
    bound_state = jnp.dot(choose, entering, precision=HIGH) + jnp.dot(
        slot_pick.astype(BF),
        partial.astype(BF).reshape(n_ctx * SLOTS, -1),
        preferred_element_type=F32,
    )
    seeds = jnp.dot(parent_hit.astype(F32), bound_state, precision=HIGH).reshape(
        n_ctx, BR_PER * rows, n_state
    )
    back = jnp.concatenate([entering.reshape(n_ctx, rows, n_state), seeds], axis=1).astype(BF)
    back = lax.all_to_all(back, "ctx", 0, 0, tiled=True)
    row = jnp.arange(length, dtype=jnp.int32)
    mixed = intra(values, b_rows, c_rows, step, cumulative, row[None, :] <= row[:, None])
    inside = (row[None, :] >= my_start[:, None]) & (row[None, :] < (my_start + my_len)[:, None])
    live = inside[0] | inside[1]
    segment = jnp.where(inside[0], 0, jnp.where(inside[1], 1, BR_PER))
    offset = row - jnp.sum(jnp.where(inside, my_start[:, None], 0), axis=0)
    tail_rows = jnp.sum(tails, axis=0).astype(BF).reshape(BR_PER * tail, row_width)
    branch_joined = jnp.concatenate([branch_x, gathered[:, width:]], axis=1)
    column = jnp.arange(BR_PER * tail, dtype=jnp.int32)
    lagged = []
    for shift in range(tail, 0, -1):
        shifted = jnp.concatenate(
            [jnp.zeros((shift, row_width), BF), branch_joined[: length - shift]], axis=0
        )
        local = jnp.where((offset >= shift)[:, None], shifted, jnp.zeros_like(shifted))
        picker = (
            (segment[:, None] == (column // tail)[None, :])
            & (offset[:, None] < shift)
            & ((column % tail)[None, :] == tail - shift + offset[:, None])
        ).astype(BF)
        lagged.append(local + jnp.dot(picker, tail_rows, preferred_element_type=F32).astype(BF))
    lagged.append(branch_joined)
    b_values, b_b, b_c = split_conv(conv_silu(lagged, weights), channels, heads)
    b_step, b_log, b_cum = decays(branch_dt, decay_rate)
    mask = (segment[:, None] == segment[None, :]) & live[:, None] & (row[None, :] <= row[:, None])
    b_mixed = intra(b_values, b_b, b_c, b_step, b_cum, mask)
    starts = pick(b_cum - b_log, my_start)
    gap = b_cum - jnp.where(inside[0][None, :], starts[0][:, None], starts[1][:, None])
    seed_weight = jnp.where(live[None, :], jnp.exp(jnp.where(live[None, :], gap, 0.0)), 0.0)
    shape = (heads, channels // heads, n_state)
    mixed = mixed + from_state(c_rows, back[:, :rows].reshape(shape), jnp.exp(cumulative))
    for slot in range(BR_PER):
        seed = back[:, (slot + 1) * rows : (slot + 2) * rows].reshape(shape)
        b_mixed = b_mixed + from_state(
            b_c, seed, jnp.where(inside[slot][None, :], seed_weight, 0.0)
        )

    def gate(mixed, values, z):
        mixed = mixed + skip[None, :, None] * values.astype(F32)
        gated = mixed.reshape(length, -1) * jax.nn.silu(z.astype(F32))
        return (gated, jnp.sum(gated * gated, axis=1))

    gated, squares = gate(mixed, values, prefix_z)
    b_gated, b_squares = gate(b_mixed, b_values, branch_z)
    every = lax.all_gather(jnp.stack([squares, b_squares])[None], "tp", axis=0, tiled=True)
    factor = lax.rsqrt(jnp.sum(every, axis=0) / (channels * lax.axis_size("tp")) + EPSILON)
    prefix_out = (gated * factor[0][:, None] * norm_gain[None, :]).astype(BF)
    branch_out = (b_gated * factor[1][:, None] * norm_gain[None, :]).astype(BF)
    return (prefix_out, jnp.where(live[:, None], branch_out, jnp.zeros_like(branch_out)))


def solution(mesh):
    both = P(("ctx", "tp"), None)
    in_specs = (
        P("ctx", "tp"),
        P("ctx", "tp"),
        both,
        P("tp", "ctx"),
        P("ctx", "tp"),
        P("ctx", "tp"),
        both,
        P("tp", "ctx"),
        P(None, "tp"),
        P(),
        P("tp"),
        P("tp"),
        P("tp"),
        P(),
        P(),
        P(),
        P(),
    )
    out_specs = (P("ctx", "tp"), P("ctx", "tp"))
    return jax.shard_map(body, mesh=mesh, in_specs=in_specs, out_specs=out_specs, check_vma=False)
```

profile of v0, /device:TPU:1, one launch (start us, length us, event | category | flops | bytes accessed | tf_op | source)
XLA Modules:
  0.0 158.5 jit_solution(17156961118969503318)
XLA Ops:
  0.6 0.8 pad_maximum_fusion.3
  1.4 25.2 %all_gather.6 = bf16[256,512]{1,0:T(8,128)(2,1)S(1)} all-gather(bf16[16,512]{1,0:T(8,128)(2,1)S(1)} %pad_maximum_fusion.3), channel_id=1, replica_groups=mesh['ctx'=32,'tp'=16] {'tp'}, dimensions={0}, use_global_device_ids=true | all-gather | bytes 278528 | tf_op jit(solution)/shard_map/all_gather | solution.py:109
  26.6 0.7 fusion.90
  27.3 3.2 %collective-permute-start = (bf16[3,768]{1,0:T(4,128)(2,1)S(1)}, bf16[3,768]{1,0:T(4,128)(2,1)S(1)}, u32[]{:S(2)}, u32[]{:S(2)}) collective-permute-start(bf16[3,768]{1,0:T(4,128)(2,1)S(1)} %fusion.90), channel_id=1, source_target_pairs={{0,16},{16,32},{32,48},{48,64},{64,80},{80,96},{96,112},{112,128},... | collective-permute-start | bytes 13832 | tf_op jit(solution)/shard_map/ppermute | solution.py:113
  33.1 1.3 compare_select_fusion.1
  34.4 1.5 bitcast_exponential_fusion
  36.0 0.7 constant_dynamic-update-slice_fusion.1
  36.7 1.4 select_reduce_fusion.2
  38.8 0.8 select_reduce_fusion.3
  40.1 0.7 constant_dynamic-update-slice_fusion
  40.9 0.7 broadcast_and_fusion
  43.1 1.0 maximum_maximum_fusion
  45.0 0.8 fusion
  46.0 0.7 fusion.44
  47.7 3.7 %concatenate.39 = bf16[32,199,128]{2,1,0:T(8,128)(2,1)S(1)} concatenate(bf16[32,16,128]{2,1,0:T(8,128)(2,1)} %get-tuple-element.25, bf16[32,16,128]{2,1,0:T(8,128)(2,1)} %get-tuple-element.24, bf16[32,128,128]{2,1,0:T(8,128)(2,1)S(1)} %bitcast.88, bf16[32,36,128]{2,1,0:T(8,128)(2,1)S(1)} %reshape.471, bf16[32,1,128]{2,1,0:T(2,128)(2,1)S(1)} %copy.56, bf16[32,1,128]{2,1,0:T(2,128)(2,1)} %copy.57, ...), dimensions={1} | concatenate | bytes 3260416 | tf_op jit(solution)/shard_map/concatenate | solution.py:165
  51.4 1.3 pad.12
  52.7 8.9 %all-to-all-start = ((bf16[32,208,128]{2,1,0:T(8,128)(2,1)}), bf16[32,208,128]{2,1,0:T(8,128)(2,1)S(1)}, u32[]{:S(2)}, u32[]{:S(2)}) async-start(bf16[32,208,128]{2,1,0:T(8,128)(2,1)} %pad.12), calls=%async_computation | async-start | bytes 3407872 | tf_op jit(solution)/shard_map/all_to_all | solution.py:167
  61.7 0.7 and.137
  64.8 0.8 fusion.41
  65.5 0.8 fusion.42
  66.3 0.8 fusion.40
  68.3 0.7 fusion.92
  69.0 0.8 and_and_fusion
  69.7 0.9 fusion.59
  70.6 31.0 %all-to-all-done = bf16[32,208,128]{2,1,0:T(8,128)(2,1)S(1)} async-done(((bf16[32,208,128]{2,1,0:T(8,128)(2,1)}), bf16[32,208,128]{2,1,0:T(8,128)(2,1)S(1)}, u32[]{:S(2)}, u32[]{:S(2)}) %all-to-all-start) | async-done | bytes 1703968 | tf_op jit(solution)/shard_map/all_to_all | solution.py:167
  103.0 1.1 slice.184
  104.1 1.5 reshape.475
  105.7 1.4 select_reduce_fusion.5
  107.0 1.4 copy.59
  108.4 0.8 subtract_reduce_fusion
  109.2 0.9 select_reduce_fusion
  110.2 1.1 fusion.46
  112.0 0.9 fusion.99
  112.9 0.9 convolution_add_fusion
  114.4 0.9 copy.66
  115.3 0.8 pad_maximum_fusion.2
  116.1 7.5 %all-to-all-start.1 = ((bf16[32,48,128]{2,1,0:T(8,128)(2,1)}), bf16[32,48,128]{2,1,0:T(8,128)(2,1)S(1)}, u32[]{:S(2)}, u32[]{:S(2)}) async-start(bf16[32,48,128]{2,1,0:T(8,128)(2,1)} %pad_maximum_fusion.2), calls=%async_computation.1 | async-start | bytes 786432 | tf_op jit(solution)/shard_map/all_to_all | solution.py:205
  123.7 1.5 fusion.16
  125.2 1.1 fusion.19
  126.4 0.7 multiply_convert_fusion.2
  127.2 0.8 copy.61
  128.0 0.9 fusion.52
  128.9 5.3 %all-to-all-done.1 = bf16[32,48,128]{2,1,0:T(8,128)(2,1)S(1)} async-done(((bf16[32,48,128]{2,1,0:T(8,128)(2,1)}), bf16[32,48,128]{2,1,0:T(8,128)(2,1)S(1)}, u32[]{:S(2)}, u32[]{:S(2)}) %all-to-all-start.1) | async-done | bytes 393248 | tf_op jit(solution)/shard_map/all_to_all | solution.py:205
  134.5 0.8 fusion.6
  136.4 0.8 fusion.7
  137.9 18.7 %all-gather.1 = f32[16,2,256]{2,1,0:T(2,128)S(1)} all-gather(f32[1,2,256]{2,1,0:T(2,128)S(1)} %maximum_bitcast_fusion), channel_id=2, replica_groups=mesh['ctx'=32,'tp'=16] {'tp'}, dimensions={0}, use_global_device_ids=true | all-gather | bytes 34816 | tf_op jit(solution)/shard_map/all_gather | solution.py:250
  156.7 0.9 fusion.45
  157.6 0.9 multiply_convert_fusion.5
  (184 shorter events, 15.6 us)
Async XLA Ops:
  0.6 43.6 %copy-start.1 = (bf16[256,512]{1,0:T(8,128)(2,1)S(1)}, bf16[256,512]{1,0:T(8,128)(2,1)}, u32[]{:S(2)}) copy-start(bf16[256,512]{1,0:T(8,128)(2,1)} %param.17) | copy-start | bytes 786436
  27.3 15.8 %collective-permute-start = (bf16[3,768]{1,0:T(4,128)(2,1)S(1)}, bf16[3,768]{1,0:T(4,128)(2,1)S(1)}, u32[]{:S(2)}, u32[]{:S(2)}) collective-permute-start(bf16[3,768]{1,0:T(4,128)(2,1)S(1)} %fusion.90), channel_id=1, source_target_pairs={{0,16},{16,32},{32,48},{48,64},{64,80},{80,96},{96,112},{112,128},... | collective-permute-start | bytes 13832 | tf_op jit(solution)/shard_map/ppermute | solution.py:113
  31.2 8.6 %copy-start.30 = (s32[8]{0:T(128)}, s32[8]{0:T(128)S(1)}, u32[]{:S(2)}) copy-start(s32[8]{0:T(128)S(1)} %get-tuple-element.16) | copy-start | bytes 100
  32.1 12.1 %copy-start.34 = (pred[8,32]{1,0:T(8,128)(4,1)}, pred[8,32]{1,0:T(8,128)(4,1)S(1)}, u32[]{:S(2)}) copy-start(pred[8,32]{1,0:T(8,128)(4,1)S(1)} %iota_compare_fusion.14) | copy-start | bytes 772
  32.2 12.0 %copy-start.35 = (pred[8,8]{1,0:T(8,128)(4,1)}, pred[8,8]{1,0:T(8,128)(4,1)S(1)}, u32[]{:S(2)}) copy-start(pred[8,8]{1,0:T(8,128)(4,1)S(1)} %iota_compare_fusion.13) | copy-start | bytes 196
  33.1 2.8 %copy-start.51 = (f32[8]{0:T(128)}, f32[8]{0:T(128)S(1)}, u32[]{:S(2)}) copy-start(f32[8]{0:T(128)S(1)} %neg.27) | copy-start | bytes 100
  36.0 8.7 %copy-start.20 = (f32[8,256]{1,0:T(8,128)}, f32[8,256]{1,0:T(8,128)S(1)}, u32[]{:S(2)}) copy-start(f32[8,256]{1,0:T(8,128)S(1)} %get-tuple-element.54) | copy-start | bytes 24580
  41.7 3.0 %copy-start.14 = (f32[768]{0:T(1024)}, f32[768]{0:T(1024)S(1)}, u32[]{:S(2)}) copy-start(f32[768]{0:T(1024)S(1)} %get-tuple-element.4) | copy-start | bytes 9220
  41.7 3.0 %copy-start.16 = (f32[768]{0:T(1024)}, f32[768]{0:T(1024)S(1)}, u32[]{:S(2)}) copy-start(f32[768]{0:T(1024)S(1)} %get-tuple-element.5) | copy-start | bytes 9220
  41.7 3.0 %copy-start.24 = (f32[768]{0:T(1024)}, f32[768]{0:T(1024)S(1)}, u32[]{:S(2)}) copy-start(f32[768]{0:T(1024)S(1)} %get-tuple-element.2) | copy-start | bytes 9220
  41.7 3.0 %copy-start.26 = (f32[768]{0:T(1024)}, f32[768]{0:T(1024)S(1)}, u32[]{:S(2)}) copy-start(f32[768]{0:T(1024)S(1)} %get-tuple-element.3) | copy-start | bytes 9220
  52.7 9.0 %copy-start.11 = (pred[8,32,8]{2,1,0:T(8,128)(4,1)S(1)}, pred[8,32,8]{2,1,0:T(8,128)(4,1)}, u32[]{:S(2)}) copy-start(pred[8,32,8]{2,1,0:T(8,128)(4,1)} %broadcast_and_fusion) | copy-start | bytes 6148
  52.7 9.7 %copy-start.42 = (s32[64]{0:T(128)S(1)}, s32[64]{0:T(128)}, u32[]{:S(2)}) copy-start(s32[64]{0:T(128)} %param.33) | copy-start | bytes 772
  52.7 9.7 %copy-start.43 = (s32[64]{0:T(128)S(1)}, s32[64]{0:T(128)}, u32[]{:S(2)}) copy-start(s32[64]{0:T(128)} %get-tuple-element.11) | copy-start | bytes 772
  52.7 9.7 %copy-start.46 = (s32[64]{0:T(128)S(1)}, s32[64]{0:T(128)}, u32[]{:S(2)}) copy-start(s32[64]{0:T(128)} %copy-done.45) | copy-start | bytes 772
  52.7 10.6 %copy-start.49 = (f32[8,256]{1,0:T(8,128)S(1)}, f32[8,256]{1,0:T(8,128)}, u32[]{:S(2)}) copy-start(f32[8,256]{1,0:T(8,128)} %param.24) | copy-start | bytes 24580
  52.7 10.6 %copy-start.52 = (f32[8]{0:T(128)S(1)}, f32[8]{0:T(128)}, u32[]{:S(2)}) copy-start(f32[8]{0:T(128)} %copy-done.51) | copy-start | bytes 100
  52.7 12.0 %copy-start = (bf16[256,512]{1,0:T(8,128)(2,1)S(1)}, bf16[256,512]{1,0:T(8,128)(2,1)}, u32[]{:S(2)}) copy-start(bf16[256,512]{1,0:T(8,128)(2,1)} %param.21) | copy-start | bytes 786436
  52.7 48.9 %all-to-all-start = ((bf16[32,208,128]{2,1,0:T(8,128)(2,1)}), bf16[32,208,128]{2,1,0:T(8,128)(2,1)S(1)}, u32[]{:S(2)}, u32[]{:S(2)}) async-start(bf16[32,208,128]{2,1,0:T(8,128)(2,1)} %pad.12), calls=%async_computation | async-start | bytes 3407872 | tf_op jit(solution)/shard_map/all_to_all | solution.py:167
  62.7 40.3 %copy-start.36 = (pred[256]{0:T(512)(128)(4,1)}, pred[256]{0:T(512)(128)(4,1)S(1)}, u32[]{:S(2)}) copy-start(pred[256]{0:T(512)(128)(4,1)S(1)} %or.10) | copy-start | bytes 772
  64.0 39.1 %copy-start.32 = (f32[8,256]{1,0:T(8,128)}, f32[8,256]{1,0:T(8,128)S(1)}, u32[]{:S(2)}) copy-start(f32[8,256]{1,0:T(8,128)S(1)} %get-tuple-element.52) | copy-start | bytes 24580
  67.1 35.9 %copy-start.22 = (s32[256]{0:T(256)}, s32[256]{0:T(256)S(1)}, u32[]{:S(2)}) copy-start(s32[256]{0:T(256)S(1)} %select_select_fusion.1) | copy-start | bytes 3076
  108.4 5.4 %copy-start.41 = (s32[64]{0:T(128)S(1)}, s32[64]{0:T(128)}, u32[]{:S(2)}) copy-start(s32[64]{0:T(128)} %copy-done.40) | copy-start | bytes 772
  112.9 10.8 %copy-start.17 = (f32[768]{0:T(1024)S(1)}, f32[768]{0:T(1024)}, u32[]{:S(2)}) copy-start(f32[768]{0:T(1024)} %copy-done.16) | copy-start | bytes 9220
  112.9 10.8 %copy-start.23 = (s32[256]{0:T(256)S(1)}, s32[256]{0:T(256)}, u32[]{:S(2)}) copy-start(s32[256]{0:T(256)} %copy-done.22) | copy-start | bytes 3076
  113.8 11.4 %copy-start.2 = (bf16[255,768]{1,0:T(8,128)(2,1)S(1)}, bf16[255,768]{1,0:T(8,128)(2,1)}, u32[]{:S(2)}) copy-start(bf16[255,768]{1,0:T(8,128)(2,1)} %fusion.42) | copy-start | bytes 1175044
  113.8 11.4 %copy-start.15 = (f32[768]{0:T(1024)S(1)}, f32[768]{0:T(1024)}, u32[]{:S(2)}) copy-start(f32[768]{0:T(1024)} %copy-done.14) | copy-start | bytes 9220
  115.3 11.0 %copy-start.25 = (f32[768]{0:T(1024)S(1)}, f32[768]{0:T(1024)}, u32[]{:S(2)}) copy-start(f32[768]{0:T(1024)} %copy-done.24) | copy-start | bytes 9220
  116.1 10.2 %copy-start.27 = (f32[768]{0:T(1024)S(1)}, f32[768]{0:T(1024)}, u32[]{:S(2)}) copy-start(f32[768]{0:T(1024)} %copy-done.26) | copy-start | bytes 9220
  116.1 10.2 %copy-start.38 = (s32[6]{0:T(128)S(1)}, s32[6]{0:T(128)}, u32[]{:S(2)}) copy-start(s32[6]{0:T(128)} %get-tuple-element.55) | copy-start | bytes 76
  116.1 10.2 %copy-start.39 = (s32[6]{0:T(128)S(1)}, s32[6]{0:T(128)}, u32[]{:S(2)}) copy-start(s32[6]{0:T(128)} %get-tuple-element.56) | copy-start | bytes 76
  116.1 10.2 %copy-start.44 = (s32[256]{0:T(256)S(1)}, s32[256]{0:T(256)}, u32[]{:S(2)}) copy-start(s32[256]{0:T(256)} %get-tuple-element.43) | copy-start | bytes 3076
  116.1 10.2 %copy-start.47 = (pred[256]{0:T(512)(128)(4,1)S(1)}, pred[256]{0:T(512)(128)(4,1)}, u32[]{:S(2)}) copy-start(pred[256]{0:T(512)(128)(4,1)} %get-tuple-element.37) | copy-start | bytes 772
  116.1 10.2 %copy-start.48 = (pred[256]{0:T(512)(128)(4,1)S(1)}, pred[256]{0:T(512)(128)(4,1)}, u32[]{:S(2)}) copy-start(pred[256]{0:T(512)(128)(4,1)} %get-tuple-element.38) | copy-start | bytes 772
  116.1 18.0 %all-to-all-start.1 = ((bf16[32,48,128]{2,1,0:T(8,128)(2,1)}), bf16[32,48,128]{2,1,0:T(8,128)(2,1)S(1)}, u32[]{:S(2)}, u32[]{:S(2)}) async-start(bf16[32,48,128]{2,1,0:T(8,128)(2,1)} %pad_maximum_fusion.2), calls=%async_computation.1 | async-start | bytes 786432 | tf_op jit(solution)/shard_map/all_to_all | solution.py:205
  123.7 2.7 %copy-start.7 = (bf16[253,768]{1,0:T(8,128)(2,1)S(1)}, bf16[253,768]{1,0:T(8,128)(2,1)}, u32[]{:S(2)}) copy-start(bf16[253,768]{1,0:T(8,128)(2,1)} %fusion.40) | copy-start | bytes 1165828
  127.1 7.1 %copy-start.28 = (f32[256,8]{0,1:T(8,128)S(1)}, f32[256,8]{0,1:T(8,128)}, u32[]{:S(2)}) copy-start(f32[256,8]{0,1:T(8,128)} %get-tuple-element.53) | copy-start | bytes 24580
  127.1 7.4 %copy-start.6 = (bf16[256,512]{0,1:T(8,128)(2,1)S(1)}, bf16[256,512]{0,1:T(8,128)(2,1)}, u32[]{:S(2)}) copy-start(bf16[256,512]{0,1:T(8,128)(2,1)} %copy-done.5) | copy-start | bytes 786436
  127.1 7.4 %copy-start.8 = (f32[256,256]{1,0:T(8,128)S(1)}, f32[256,256]{1,0:T(8,128)}, u32[]{:S(2)}) copy-start(f32[256,256]{1,0:T(8,128)} %fusion.59) | copy-start | bytes 786436
  127.1 7.4 %copy-start.12 = (pred[256,256]{1,0:T(8,128)(4,1)S(1)}, pred[256,256]{1,0:T(8,128)(4,1)}, u32[]{:S(2)}) copy-start(pred[256,256]{1,0:T(8,128)(4,1)} %iota_compare_fusion.5) | copy-start | bytes 196612
  127.1 7.4 %copy-start.21 = (f32[8,256]{1,0:T(8,128)S(1)}, f32[8,256]{1,0:T(8,128)}, u32[]{:S(2)}) copy-start(f32[8,256]{1,0:T(8,128)} %copy-done.20) | copy-start | bytes 24580
  127.1 7.4 %copy-start.31 = (f32[8,256]{1,0:T(8,128)S(1)}, f32[8,256]{1,0:T(8,128)}, u32[]{:S(2)}) copy-start(f32[8,256]{1,0:T(8,128)} %get-tuple-element.31) | copy-start | bytes 24580
  127.1 7.4 %copy-start.50 = (f32[8]{0:T(128)S(1)}, f32[8]{0:T(128)}, u32[]{:S(2)}) copy-start(f32[8]{0:T(128)} %param.28) | copy-start | bytes 100
  134.5 1.1 copy-start.19
  134.5 1.3 copy-start.18
  136.3 1.3 copy-start.3
  137.2 19.5 %copy-start.29 = (f32[512]{0:T(512)S(1)}, f32[512]{0:T(512)}, u32[]{:S(2)}) copy-start(f32[512]{0:T(512)} %param.29) | copy-start | bytes 6148
  137.2 19.5 %copy-start.37 = (pred[256]{0:T(512)(128)(4,1)S(1)}, pred[256]{0:T(512)(128)(4,1)}, u32[]{:S(2)}) copy-start(pred[256]{0:T(512)(128)(4,1)} %copy-done.36) | copy-start | bytes 772
  (9 other events, 8.2 us)
where the time goes:
time: 160 us; the launch traced here: 158 us
  blocking collectives  43.9 us (27%)
  waiting for transfers between devices  36.3 us (23%)
  other arithmetic  25.4 us (16%)
  starting transfers between devices  19.6 us (12%)
  local copies, waits for them, and re-layouts  17.9 us (11%)
  matrix products  13.9 us (9%)
    all_to_all x1, waiting for transfers between devices, body(): got = lax.all_to_all(sent, 'ctx', 0, 0, tiled=True)  31 us
    all_gather x1, blocking collectives, body(): lax.all_gather(jnp.concatenate([prefix_bc, branch_bc], axis=1), 'tp', axi...  25.2 us
    all_gather x1, blocking collectives, body(): lax.all_gather(jnp.stack([squares, b_squares])[None], 'tp', axis=0, tiled...  18.7 us
    all_to_all x1, starting transfers between devices, body(): got = lax.all_to_all(sent, 'ctx', 0, 0, tiled=True)  8.92 us
    all_to_all x1, starting transfers between devices, body(): back = lax.all_to_all(back, 'ctx', 0, 0, tiled=True)  7.45 us
    all_to_all x1, waiting for transfers between devices, body(): back = lax.all_to_all(back, 'ctx', 0, 0, tiled=True)  5.25 us
    concatenate x1, local copies, waits for them, and re-layouts, body(): sent = jnp.concatenate(pieces, axis=1)  3.65 us
    dot_general x3, matrix products, body(): jnp.dot(picker, tail_rows, preferred_element_type=F32).astype(BF)  3.24 us
  transfers between devices with their start and end apart: 3, of which 2 were waited for; matrix products, arithmetic and copies ran while one was open for 17% of the time, Pallas kernels for 0%

commit v1 on v0

--- a/solution.py
+++ b/solution.py
@@ -106,8 +106,9 @@
     taps = weights.shape[0]
     tail = taps - 1
     row_width = channels + width
-    gathered = lax.all_gather(
-        jnp.concatenate([prefix_bc, branch_bc], axis=1), "tp", axis=0, tiled=True
+    patch = jnp.concatenate([prefix_bc, branch_bc], axis=1)
+    gathered = jnp.concatenate(
+        lax.all_to_all(jnp.stack(lax.axis_size("tp") * [patch]), "tp", 0, 0), axis=0
     )
     joined = jnp.concatenate([prefix_x, gathered[:, :width]], axis=1)
     before = lax.ppermute(joined[length - tail :], "ctx", [(i, i + 1) for i in range(n_ctx - 1)])

time: 160 us -> 148 us (0.925)
  blocking collectives: 43.9 us -> 20.4 us
  starting transfers between devices: 19.6 us -> 34.3 us
  matrix products: 13.9 us -> 17.2 us
  other arithmetic: 25.4 us -> 23.2 us
  local copies, waits for them, and re-layouts: 17.9 us -> 15.8 us
    all_gather x1 -> x0, blocking collectives: 25.2 us -> none  [body(): lax.all_gather(jnp.concatenate([prefix_bc, branch_bc], axis=1), 'tp', axi...]
    all_to_all x0 -> x1, starting transfers between devices: none -> 11.8 us  [body(): lax.all_to_all(jnp.stack(lax.axis_size('tp') * [patch]), 'tp', 0, 0)]
    all_to_all x1, starting transfers between devices: 8.92 us -> 11.8 us  [body(): got = lax.all_to_all(sent, 'ctx', 0, 0, tiled=True)]
    all_to_all x1, waiting for transfers between devices: 5.25 us -> 2.65 us  [body(): back = lax.all_to_all(back, 'ctx', 0, 0, tiled=True)]
    concatenate x1, local copies, waits for them, and re-layouts: 3.65 us -> 1.13 us  [body(): sent = jnp.concatenate(pieces, axis=1)]
    all_gather x1, blocking collectives: 18.7 us -> 20.4 us  [body(): lax.all_gather(jnp.stack([squares, b_squares])[None], 'tp', axis=0, tiled...]
    dot_general x3, matrix products: 0.67 us -> 2.34 us  [from_state(): jnp.einsum('tn,hpn->thp', c_rows, state, preferred_element_type=F32)]
  transfers between devices with their start and end apart: 3 -> 4, of which waited for: 2 -> 4; matrix products, arithmetic and copies ran while one was open for 17% -> 18% of each run, Pallas kernels for 0% -> 0%
where the time goes in v1:
time: 148 us; the launch traced here: 147 us
  waiting for transfers between devices  34.9 us (24%)
  starting transfers between devices  34.3 us (23%)
  other arithmetic  23.2 us (16%)
  blocking collectives  20.4 us (14%)
  matrix products  17.2 us (12%)
  local copies, waits for them, and re-layouts  15.8 us (11%)
  between operations  1.59 us (1%)
    all_to_all x1, waiting for transfers between devices, body(): got = lax.all_to_all(sent, 'ctx', 0, 0, tiled=True)  30.9 us
    all_gather x1, blocking collectives, body(): lax.all_gather(jnp.stack([squares, b_squares])[None], 'tp', axis=0, tiled...  20.4 us
    all_to_all x1, starting transfers between devices, body(): lax.all_to_all(jnp.stack(lax.axis_size('tp') * [patch]), 'tp', 0, 0)  11.8 us
    all_to_all x1, starting transfers between devices, body(): got = lax.all_to_all(sent, 'ctx', 0, 0, tiled=True)  11.8 us
    all_to_all x1, starting transfers between devices, body(): back = lax.all_to_all(back, 'ctx', 0, 0, tiled=True)  7.47 us
    dot_general x3, matrix products, body(): jnp.dot(picker, tail_rows, preferred_element_type=F32).astype(BF)  4.01 us
    ppermute x1, starting transfers between devices, body(): lax.ppermute(joined[length - tail:], 'ctx', [(i, i + 1) for i in range(n_...  3.2 us
  transfers between devices with their start and end apart: 4, of which 4 were waited for; matrix products, arithmetic and copies ran while one was open for 18% of the time, Pallas kernels for 0%

profile of v1, /device:TPU:1, one launch (start us, length us, event | category | flops | bytes accessed | tf_op | source)
XLA Modules:
  0.0 147.3 jit_solution(5981731337357208059)
XLA Ops:
  0.6 0.8 pad_maximum_fusion.3
  1.4 0.7 stack.8
  2.1 11.8 %all-to-all-start = ((bf16[16,16,512]{2,1,0:T(8,128)(2,1)}), bf16[16,16,512]{2,1,0:T(8,128)(2,1)S(1)}, u32[]{:S(2)}, u32[]{:S(2)}) async-start(bf16[16,16,512]{2,1,0:T(8,128)(2,1)} %stack.8), calls=%async_computation | async-start | bytes 524288 | tf_op jit(solution)/shard_map/all_to_all | solution.py:111
  16.6 1.3 compare_select_fusion.1
  17.9 1.5 %bitcast_exponential_fusion = (f32[256,8]{0,1:T(8,128)}, f32[8,256]{1,0:T(8,128)S(1)}) fusion(f32[8]{0:T(128)S(1)} %neg.27, f32[8,256]{1,0:T(8,128)} %param.20), kind=kOutput, calls=%fused_computation.253 | convolution fusion | flops 6371328 | bytes 24608 | tf_op jit(solution)/shard_map/dot_general | solution.py:34
  20.1 0.9 select_reduce_fusion.2
  21.7 0.8 select_reduce_fusion.3
  23.2 0.7 broadcast_and_fusion
  24.8 0.8 all-to-all-done
  25.7 0.7 fusion.90
  26.4 3.2 %collective-permute-start = (bf16[3,768]{1,0:T(4,128)(2,1)S(1)}, bf16[3,768]{1,0:T(4,128)(2,1)S(1)}, u32[]{:S(2)}, u32[]{:S(2)}) collective-permute-start(bf16[3,768]{1,0:T(4,128)(2,1)S(1)} %fusion.90), channel_id=1, source_target_pairs={{0,16},{16,32},{32,48},{48,64},{64,80},{80,96},{96,112},{112,128},... | collective-permute-start | bytes 13832 | tf_op jit(solution)/shard_map/ppermute | solution.py:114
  31.2 0.8 fusion
  33.3 1.1 concatenate.39
  34.4 1.3 pad.12
  35.8 11.8 %all-to-all-start.1 = ((bf16[32,208,128]{2,1,0:T(8,128)(2,1)}), bf16[32,208,128]{2,1,0:T(8,128)(2,1)S(1)}, u32[]{:S(2)}, u32[]{:S(2)}) async-start(bf16[32,208,128]{2,1,0:T(8,128)(2,1)} %pad.12), calls=%async_computation.1 | async-start | bytes 3407872 | tf_op jit(solution)/shard_map/all_to_all | solution.py:168
  47.6 0.7 and.137
  52.5 0.8 and_and_fusion
  53.3 0.8 fusion.41
  54.1 0.8 fusion.42
  54.9 0.8 fusion.40
  55.6 0.9 fusion.59
  56.6 30.9 %all-to-all-done.1 = bf16[32,208,128]{2,1,0:T(8,128)(2,1)S(1)} async-done(((bf16[32,208,128]{2,1,0:T(8,128)(2,1)}), bf16[32,208,128]{2,1,0:T(8,128)(2,1)S(1)}, u32[]{:S(2)}, u32[]{:S(2)}) %all-to-all-start.1) | async-done | bytes 1703968 | tf_op jit(solution)/shard_map/all_to_all | solution.py:168
  88.9 1.1 slice.184
  90.0 1.5 %reshape.481 = bf16[256,2048]{1,0:T(8,128)(2,1)S(1)} reshape(bf16[32,128,128]{2,1,0:T(8,128)(2,1)} %slice.184) | data formatting | bytes 2097152 | tf_op jit(solution)/shard_map/reshape | solution.py:199
  91.5 1.3 select_reduce_fusion.5
  92.8 1.3 copy.59
  94.1 0.8 subtract_reduce_fusion
  94.9 0.9 select_reduce_fusion
  95.9 1.0 fusion.46
  97.6 0.9 fusion.99
  98.5 0.9 convolution_add_fusion
  100.0 0.9 copy.66
  101.0 0.8 pad_maximum_fusion.2
  101.8 7.5 %all-to-all-start.2 = ((bf16[32,48,128]{2,1,0:T(8,128)(2,1)}), bf16[32,48,128]{2,1,0:T(8,128)(2,1)S(1)}, u32[]{:S(2)}, u32[]{:S(2)}) async-start(bf16[32,48,128]{2,1,0:T(8,128)(2,1)} %pad_maximum_fusion.2), calls=%async_computation.2 | async-start | bytes 786432 | tf_op jit(solution)/shard_map/all_to_all | solution.py:206
  109.4 1.5 fusion.16
  110.9 1.1 fusion.19
  112.1 1.5 multiply_convert_fusion.2
  113.6 1.0 slice.196
  114.6 0.8 copy.61
  115.4 1.8 %fusion.52 = f32[256,256]{1,0:T(8,128)} fusion(bf16[256,768]{1,0:T(8,128)(2,1)} %multiply_convert_fusion.2), kind=kOutput, calls=%fused_computation.101 | convolution fusion | flops 16777216 | bytes 393216 | tf_op jit(solution)/shard_map/dot_general | solution.py:38
  117.2 2.6 %all-to-all-done.2 = bf16[32,48,128]{2,1,0:T(8,128)(2,1)S(1)} async-done(((bf16[32,48,128]{2,1,0:T(8,128)(2,1)}), bf16[32,48,128]{2,1,0:T(8,128)(2,1)S(1)}, u32[]{:S(2)}, u32[]{:S(2)}) %all-to-all-start.2) | async-done | bytes 393248 | tf_op jit(solution)/shard_map/all_to_all | solution.py:206
  120.2 0.8 fusion.6
  121.2 1.1 convolution_multiply_fusion.1
  122.3 1.1 convolution_multiply_fusion
  123.5 0.8 fusion.7
  125.0 20.4 %all-gather.1 = f32[16,2,256]{2,1,0:T(2,128)S(1)} all-gather(f32[1,2,256]{2,1,0:T(2,128)S(1)} %maximum_bitcast_fusion), channel_id=2, replica_groups=mesh['ctx'=32,'tp'=16] {'tp'}, dimensions={0}, use_global_device_ids=true | all-gather | bytes 34816 | tf_op jit(solution)/shard_map/all_gather | solution.py:251
  145.5 0.9 fusion.45
  146.4 0.9 multiply_convert_fusion.5
  (180 shorter events, 16.6 us)
Async XLA Ops:
  0.6 29.7 %copy-start.1 = (bf16[256,512]{1,0:T(8,128)(2,1)S(1)}, bf16[256,512]{1,0:T(8,128)(2,1)}, u32[]{:S(2)}) copy-start(bf16[256,512]{1,0:T(8,128)(2,1)} %param.17) | copy-start | bytes 786436
  2.1 23.5 %all-to-all-start = ((bf16[16,16,512]{2,1,0:T(8,128)(2,1)}), bf16[16,16,512]{2,1,0:T(8,128)(2,1)S(1)}, u32[]{:S(2)}, u32[]{:S(2)}) async-start(bf16[16,16,512]{2,1,0:T(8,128)(2,1)} %stack.8), calls=%async_computation | async-start | bytes 524288 | tf_op jit(solution)/shard_map/all_to_all | solution.py:111
  14.6 10.1 %copy-start.32 = (s32[8]{0:T(128)}, s32[8]{0:T(128)S(1)}, u32[]{:S(2)}) copy-start(s32[8]{0:T(128)S(1)} %get-tuple-element.16) | copy-start | bytes 100
  15.6 9.2 %copy-start.36 = (pred[8,32]{1,0:T(8,128)(4,1)}, pred[8,32]{1,0:T(8,128)(4,1)S(1)}, u32[]{:S(2)}) copy-start(pred[8,32]{1,0:T(8,128)(4,1)S(1)} %iota_compare_fusion.14) | copy-start | bytes 772
  15.6 9.1 %copy-start.37 = (pred[8,8]{1,0:T(8,128)(4,1)}, pred[8,8]{1,0:T(8,128)(4,1)S(1)}, u32[]{:S(2)}) copy-start(pred[8,8]{1,0:T(8,128)(4,1)S(1)} %iota_compare_fusion.13) | copy-start | bytes 196
  19.4 7.0 %copy-start.22 = (f32[8,256]{1,0:T(8,128)}, f32[8,256]{1,0:T(8,128)S(1)}, u32[]{:S(2)}) copy-start(f32[8,256]{1,0:T(8,128)S(1)} %get-tuple-element.54) | copy-start | bytes 24580
  26.4 4.0 %collective-permute-start = (bf16[3,768]{1,0:T(4,128)(2,1)S(1)}, bf16[3,768]{1,0:T(4,128)(2,1)S(1)}, u32[]{:S(2)}, u32[]{:S(2)}) collective-permute-start(bf16[3,768]{1,0:T(4,128)(2,1)S(1)} %fusion.90), channel_id=1, source_target_pairs={{0,16},{16,32},{32,48},{48,64},{64,80},{80,96},{96,112},{112,128},... | collective-permute-start | bytes 13832 | tf_op jit(solution)/shard_map/ppermute | solution.py:114
  29.7 1.5 %copy-start.26 = (f32[768]{0:T(1024)}, f32[768]{0:T(1024)S(1)}, u32[]{:S(2)}) copy-start(f32[768]{0:T(1024)S(1)} %get-tuple-element.2) | copy-start | bytes 9220
  29.7 1.5 %copy-start.16 = (f32[768]{0:T(1024)}, f32[768]{0:T(1024)S(1)}, u32[]{:S(2)}) copy-start(f32[768]{0:T(1024)S(1)} %get-tuple-element.4) | copy-start | bytes 9220
  29.7 1.5 %copy-start.18 = (f32[768]{0:T(1024)}, f32[768]{0:T(1024)S(1)}, u32[]{:S(2)}) copy-start(f32[768]{0:T(1024)S(1)} %get-tuple-element.5) | copy-start | bytes 9220
  35.7 11.8 %copy-start.13 = (pred[8,32,8]{2,1,0:T(8,128)(4,1)S(1)}, pred[8,32,8]{2,1,0:T(8,128)(4,1)}, u32[]{:S(2)}) copy-start(pred[8,32,8]{2,1,0:T(8,128)(4,1)} %broadcast_and_fusion) | copy-start | bytes 6148
  35.7 12.5 %copy-start.44 = (s32[64]{0:T(128)S(1)}, s32[64]{0:T(128)}, u32[]{:S(2)}) copy-start(s32[64]{0:T(128)} %param.33) | copy-start | bytes 772
  35.8 13.4 %copy-start.48 = (f32[8,256]{1,0:T(8,128)S(1)}, f32[8,256]{1,0:T(8,128)}, u32[]{:S(2)}) copy-start(f32[8,256]{1,0:T(8,128)} %param.24) | copy-start | bytes 24580
  35.8 17.6 %copy-start = (bf16[256,512]{1,0:T(8,128)(2,1)S(1)}, bf16[256,512]{1,0:T(8,128)(2,1)}, u32[]{:S(2)}) copy-start(bf16[256,512]{1,0:T(8,128)(2,1)} %param.21) | copy-start | bytes 786436
  35.8 51.7 %all-to-all-start.1 = ((bf16[32,208,128]{2,1,0:T(8,128)(2,1)}), bf16[32,208,128]{2,1,0:T(8,128)(2,1)S(1)}, u32[]{:S(2)}, u32[]{:S(2)}) async-start(bf16[32,208,128]{2,1,0:T(8,128)(2,1)} %pad.12), calls=%async_computation.1 | async-start | bytes 3407872 | tf_op jit(solution)/shard_map/all_to_all | solution.py:168
  47.5 8.1 %copy-start.3 = (bf16[256,768]{1,0:T(8,128)(2,1)S(1)}, bf16[256,768]{1,0:T(8,128)(2,1)}, u32[]{:S(2)}) copy-start(bf16[256,768]{1,0:T(8,128)(2,1)} %copy-done.2) | copy-start | bytes 1179652
  48.6 4.7 %copy-start.38 = (pred[256]{0:T(512)(128)(4,1)}, pred[256]{0:T(512)(128)(4,1)S(1)}, u32[]{:S(2)}) copy-start(pred[256]{0:T(512)(128)(4,1)S(1)} %or.10) | copy-start | bytes 772
  49.8 3.5 %copy-start.34 = (f32[8,256]{1,0:T(8,128)}, f32[8,256]{1,0:T(8,128)S(1)}, u32[]{:S(2)}) copy-start(f32[8,256]{1,0:T(8,128)S(1)} %get-tuple-element.52) | copy-start | bytes 24580
  50.6 1.9 %copy-start.24 = (s32[256]{0:T(256)}, s32[256]{0:T(256)S(1)}, u32[]{:S(2)}) copy-start(s32[256]{0:T(256)S(1)} %select_select_fusion.1) | copy-start | bytes 3076
  94.1 5.4 %copy-start.43 = (s32[64]{0:T(128)S(1)}, s32[64]{0:T(128)}, u32[]{:S(2)}) copy-start(s32[64]{0:T(128)} %copy-done.42) | copy-start | bytes 772
  98.5 10.8 %copy-start.19 = (f32[768]{0:T(1024)S(1)}, f32[768]{0:T(1024)}, u32[]{:S(2)}) copy-start(f32[768]{0:T(1024)} %copy-done.18) | copy-start | bytes 9220
  98.5 10.8 %copy-start.25 = (s32[256]{0:T(256)S(1)}, s32[256]{0:T(256)}, u32[]{:S(2)}) copy-start(s32[256]{0:T(256)} %copy-done.24) | copy-start | bytes 3076
  99.5 11.4 %copy-start.4 = (bf16[255,768]{1,0:T(8,128)(2,1)S(1)}, bf16[255,768]{1,0:T(8,128)(2,1)}, u32[]{:S(2)}) copy-start(bf16[255,768]{1,0:T(8,128)(2,1)} %fusion.42) | copy-start | bytes 1175044
  99.5 11.4 %copy-start.17 = (f32[768]{0:T(1024)S(1)}, f32[768]{0:T(1024)}, u32[]{:S(2)}) copy-start(f32[768]{0:T(1024)} %copy-done.16) | copy-start | bytes 9220
  101.0 11.0 %copy-start.27 = (f32[768]{0:T(1024)S(1)}, f32[768]{0:T(1024)}, u32[]{:S(2)}) copy-start(f32[768]{0:T(1024)} %copy-done.26) | copy-start | bytes 9220
  101.7 10.3 %copy-start.29 = (f32[768]{0:T(1024)S(1)}, f32[768]{0:T(1024)}, u32[]{:S(2)}) copy-start(f32[768]{0:T(1024)} %copy-done.28) | copy-start | bytes 9220
  101.7 10.3 %copy-start.40 = (s32[6]{0:T(128)S(1)}, s32[6]{0:T(128)}, u32[]{:S(2)}) copy-start(s32[6]{0:T(128)} %get-tuple-element.55) | copy-start | bytes 76
  101.7 10.3 %copy-start.41 = (s32[6]{0:T(128)S(1)}, s32[6]{0:T(128)}, u32[]{:S(2)}) copy-start(s32[6]{0:T(128)} %get-tuple-element.56) | copy-start | bytes 76
  101.7 10.3 %copy-start.45 = (s32[256]{0:T(256)S(1)}, s32[256]{0:T(256)}, u32[]{:S(2)}) copy-start(s32[256]{0:T(256)} %get-tuple-element.43) | copy-start | bytes 3076
  101.7 10.3 %copy-start.46 = (pred[256]{0:T(512)(128)(4,1)S(1)}, pred[256]{0:T(512)(128)(4,1)}, u32[]{:S(2)}) copy-start(pred[256]{0:T(512)(128)(4,1)} %get-tuple-element.37) | copy-start | bytes 772
  101.8 10.3 %copy-start.47 = (pred[256]{0:T(512)(128)(4,1)S(1)}, pred[256]{0:T(512)(128)(4,1)}, u32[]{:S(2)}) copy-start(pred[256]{0:T(512)(128)(4,1)} %get-tuple-element.38) | copy-start | bytes 772
  101.8 18.1 %all-to-all-start.2 = ((bf16[32,48,128]{2,1,0:T(8,128)(2,1)}), bf16[32,48,128]{2,1,0:T(8,128)(2,1)S(1)}, u32[]{:S(2)}, u32[]{:S(2)}) async-start(bf16[32,48,128]{2,1,0:T(8,128)(2,1)} %pad_maximum_fusion.2), calls=%async_computation.2 | async-start | bytes 786432 | tf_op jit(solution)/shard_map/all_to_all | solution.py:206
  109.3 2.7 %copy-start.9 = (bf16[253,768]{1,0:T(8,128)(2,1)S(1)}, bf16[253,768]{1,0:T(8,128)(2,1)}, u32[]{:S(2)}) copy-start(bf16[253,768]{1,0:T(8,128)(2,1)} %fusion.40) | copy-start | bytes 1165828
  113.5 6.4 %copy-start.30 = (f32[256,8]{0,1:T(8,128)S(1)}, f32[256,8]{0,1:T(8,128)}, u32[]{:S(2)}) copy-start(f32[256,8]{0,1:T(8,128)} %get-tuple-element.53) | copy-start | bytes 24580
  113.5 6.6 %copy-start.8 = (bf16[256,512]{0,1:T(8,128)(2,1)S(1)}, bf16[256,512]{0,1:T(8,128)(2,1)}, u32[]{:S(2)}) copy-start(bf16[256,512]{0,1:T(8,128)(2,1)} %copy-done.7) | copy-start | bytes 786436
  113.5 6.6 %copy-start.10 = (f32[256,256]{1,0:T(8,128)S(1)}, f32[256,256]{1,0:T(8,128)}, u32[]{:S(2)}) copy-start(f32[256,256]{1,0:T(8,128)} %fusion.59) | copy-start | bytes 786436
  113.5 6.6 %copy-start.14 = (pred[256,256]{1,0:T(8,128)(4,1)S(1)}, pred[256,256]{1,0:T(8,128)(4,1)}, u32[]{:S(2)}) copy-start(pred[256,256]{1,0:T(8,128)(4,1)} %iota_compare_fusion.5) | copy-start | bytes 196612
  113.5 6.6 %copy-start.23 = (f32[8,256]{1,0:T(8,128)S(1)}, f32[8,256]{1,0:T(8,128)}, u32[]{:S(2)}) copy-start(f32[8,256]{1,0:T(8,128)} %copy-done.22) | copy-start | bytes 24580
  113.5 6.6 %copy-start.33 = (f32[8,256]{1,0:T(8,128)S(1)}, f32[8,256]{1,0:T(8,128)}, u32[]{:S(2)}) copy-start(f32[8,256]{1,0:T(8,128)} %get-tuple-element.31) | copy-start | bytes 24580
  113.5 6.6 %copy-start.49 = (f32[8]{0:T(128)S(1)}, f32[8]{0:T(128)}, u32[]{:S(2)}) copy-start(f32[8]{0:T(128)} %param.28) | copy-start | bytes 100
  120.2 2.1 %copy-start.20 = (f32[256,8]{0,1:T(8,128)S(1)}, f32[256,8]{0,1:T(8,128)}, u32[]{:S(2)}) copy-start(f32[256,8]{0,1:T(8,128)} %get-tuple-element.30) | copy-start | bytes 24580
  121.0 2.4 %copy-start.11 = (f32[256,256]{1,0:T(8,128)S(1)}, f32[256,256]{1,0:T(8,128)}, u32[]{:S(2)}) copy-start(f32[256,256]{1,0:T(8,128)} %fusion.52) | copy-start | bytes 786436
  121.0 2.4 %copy-start.12 = (bf16[256,512]{0,1:T(8,128)(2,1)S(1)}, bf16[256,512]{0,1:T(8,128)(2,1)}, u32[]{:S(2)}) copy-start(bf16[256,512]{0,1:T(8,128)(2,1)} %copy.61) | copy-start | bytes 786436
  121.0 2.4 %copy-start.15 = (pred[256,256]{1,0:T(8,128)(4,1)S(1)}, pred[256,256]{1,0:T(8,128)(4,1)}, u32[]{:S(2)}) copy-start(pred[256,256]{1,0:T(8,128)(4,1)} %and_and_fusion) | copy-start | bytes 196612
  121.0 2.4 %copy-start.35 = (f32[8,256]{1,0:T(8,128)S(1)}, f32[8,256]{1,0:T(8,128)}, u32[]{:S(2)}) copy-start(f32[8,256]{1,0:T(8,128)} %copy-done.34) | copy-start | bytes 24580
  121.0 2.4 %copy-start.50 = (f32[8,256]{1,0:T(8,128)S(1)}, f32[8,256]{1,0:T(8,128)}, u32[]{:S(2)}) copy-start(f32[8,256]{1,0:T(8,128)} %get-tuple-element.33) | copy-start | bytes 24580
  124.2 21.2 %copy-start.31 = (f32[512]{0:T(512)S(1)}, f32[512]{0:T(512)}, u32[]{:S(2)}) copy-start(f32[512]{0:T(512)} %param.29) | copy-start | bytes 6148
  124.3 21.2 %copy-start.39 = (pred[256]{0:T(512)(128)(4,1)S(1)}, pred[256]{0:T(512)(128)(4,1)}, u32[]{:S(2)}) copy-start(pred[256]{0:T(512)(128)(4,1)} %copy-done.38) | copy-start | bytes 772
  (7 other events, 7.4 us)
